TPU v7x, 32 devices: a whole 2x2x4 slice. The times are simulated.
32 devices in a mesh: rep: 2 (over y), expert: 8 (over z, x), group: 2 (over core).
Axes of the slice: x: 2, y: 2, z: 4, core: 2. Of those that a mesh axis runs over, the one named last changes fastest.
Arguments:
- tokens: bfloat16 [4096, 1024], P(('rep', 'expert', 'group')), parts along dimension 0, may hold values from -6 to 6
- w_gate: bfloat16 [16, 1024, 384], P('expert', 'group'), may hold values from -0.1875 to 0.1875
- w_up: bfloat16 [16, 1024, 384], P('expert', 'group'), may hold values from -0.1875 to 0.1875
- w_down: bfloat16 [16, 384, 1024], P('expert', 'group'), may hold values from -0.45927933 to 0.45927933
- route_ids: int32 [4096, 8], P(('rep', 'expert', 'group')), parts along dimension 0, may hold values from 0 to 15, all different within a row; in each aligned block of 128 rows (0 to 127, 128 to 255, ...) at most 80 rows name the same one
- route_scores: float32 [4096, 8], P(('rep', 'expert', 'group')), parts along dimension 0, may hold values from 0.05 to 1
- norm_gain: float32 [1024], replicated, may hold values from 0.5 to 1.5
- class_head: bfloat16 [1024, 2000], P(None, 'expert'), may hold values from -0.59765625 to 0.59765625
- targets: int32 [16, 2, 2000], P('rep', 'group', 'expert'), parts along dimension 0, may hold values 0 or 1
Outputs:
- token_grad: bfloat16 [4096, 1024], P(('rep', 'expert', 'group')), parts along dimension 0
- head_grad: float32 [2048, 2000], P('rep', 'expert'), parts along dimension 0
There are 2 independent parts, one for each index of `rep`. A program takes and returns all parts, laid end to end along the dimension named above; an argument that names none is the same for every part. Nothing has to cross between parts.
Inputs may be any that keep to these rules, and one draw needn't show every extreme that they name: `route_ids`: each row names 8 different experts; among the 128 tokens of one sequence no expert is named by more than 80 tokens, and in some sequences one expert is named by exactly 80.
All inputs are finite; a program needn't handle non-finite values. No bound on the sum of `targets` on one device may be relied on, other than what follows from the above.
Results may differ from a plain program's by a relative error of at most 0.022.
Values may be sent and summed in bfloat16 or wider, within the bound.
A program may use at most 64 MiB of HBM per device.

v0:
```python
import jax
import jax.numpy as jnp
from jax import lax
from jax.sharding import PartitionSpec as P

LOSS_SCALE = 8.0
NORM_EPS = 1e-06


def body(tokens, w_gate, w_up, w_down, route_ids, route_scores, norm_gain, class_head, targets):
    rows_here, feature_dim = tokens.shape
    top_count = route_ids.shape[1]
    expert_count = lax.axis_size("expert")
    local_experts = w_gate.shape[0]
    experts_all = expert_count * local_experts
    capacity = min(rows_here, rows_here * top_count * 5 // (4 * experts_all))
    route_weight = route_scores / jnp.sum(route_scores, axis=-1, keepdims=True)
    expert_iota = jnp.arange(experts_all, dtype=jnp.int32)
    named_count = jnp.zeros((rows_here, experts_all), jnp.int32)
    for choice_k in range(top_count):
        named_count = named_count + (
            route_ids[:, choice_k][:, None] == expert_iota[None, :]
        ).astype(jnp.int32)
    before = jnp.cumsum(named_count, axis=0) - named_count
    position_cols = []
    for choice_k in range(top_count):
        hit_expert = route_ids[:, choice_k][:, None] == expert_iota[None, :]
        position_cols.append(jnp.sum(jnp.where(hit_expert, before, 0), axis=1))
    position = jnp.stack(position_cols, axis=1)
    slot_index = route_ids * capacity + position
    slot_iota = jnp.arange(experts_all * capacity, dtype=jnp.int32)
    place_rows = jnp.zeros((experts_all * capacity, rows_here), jnp.float32)
    place_weight = jnp.zeros((experts_all * capacity, rows_here), jnp.float32)
    for choice_k in range(top_count):
        slot_hit = slot_iota[:, None] == slot_index[:, choice_k][None, :]
        place_rows = place_rows + slot_hit.astype(jnp.float32)
        place_weight = place_weight + jnp.where(slot_hit, route_weight[:, choice_k][None, :], 0.0)
    place_rows = place_rows.astype(jnp.bfloat16)
    slot_shape = (expert_count, local_experts, capacity, feature_dim)
    outgoing = (
        jnp.dot(place_rows, tokens, preferred_element_type=jnp.float32)
        .astype(jnp.bfloat16)
        .reshape(slot_shape)
    )
    gate_full, up_full, down_full = (
        lax.all_gather(w_gate, "group", axis=1, tiled=True),
        lax.all_gather(w_up, "group", axis=1, tiled=True),
        lax.all_gather(w_down, "group", axis=1, tiled=True),
    )
    incoming = lax.all_to_all(outgoing, "expert", split_axis=0, concat_axis=0, tiled=True)
    gate_list = []
    up_list = []
    hidden_list = []
    for local in range(local_experts):
        expert_rows = incoming[:, local].reshape(-1, feature_dim)
        gate_act = jnp.dot(expert_rows, gate_full[local], preferred_element_type=jnp.float32)
        up_act = jnp.dot(expert_rows, up_full[local], preferred_element_type=jnp.float32)
        hidden = (gate_act * jax.nn.sigmoid(gate_act) * up_act).astype(jnp.bfloat16)
        gate_list.append(gate_act)
        up_list.append(up_act)
        hidden_list.append(hidden)
    out_list = []
    for local in range(local_experts):
        expert_out = jnp.dot(
            hidden_list[local], down_full[local], preferred_element_type=jnp.float32
        ).astype(jnp.bfloat16)
        out_list.append(expert_out.reshape(expert_count, capacity, feature_dim))
    expert_out_all = jnp.stack(out_list, axis=1)
    returned = lax.all_to_all(
        expert_out_all, "expert", split_axis=0, concat_axis=0, tiled=True
    ).reshape(-1, feature_dim)
    picked = jnp.take(returned, slot_index.reshape(-1), axis=0).reshape(
        rows_here, top_count, feature_dim
    )
    moe_out = jnp.einsum("tk,tkd->td", route_weight, picked.astype(jnp.float32))
    residual = tokens.astype(jnp.float32) + moe_out
    inv_rms = lax.rsqrt(jnp.mean(residual * residual, axis=-1, keepdims=True) + NORM_EPS)
    normed = residual * inv_rms * norm_gain
    pooled = jnp.mean(normed, axis=0, keepdims=True).astype(jnp.bfloat16)
    pooled_all = lax.all_gather(pooled, "expert", axis=0, tiled=True)
    logits = jnp.dot(pooled_all, class_head, preferred_element_type=jnp.float32)
    target_rows = targets.reshape(expert_count, -1).astype(jnp.float32)
    logit_grad = (LOSS_SCALE * (jax.nn.sigmoid(logits) - target_rows)).astype(jnp.bfloat16)
    head_part = lax.dot_general(
        pooled_all, logit_grad, (((0,), (0,)), ((), ())), preferred_element_type=jnp.float32
    )
    head_grad = lax.psum(head_part.astype(jnp.bfloat16), "group").astype(jnp.float32)
    pooled_terms = lax.dot_general(
        logit_grad, class_head, (((1,), (1,)), ((), ())), preferred_element_type=jnp.float32
    )
    pooled_grad = lax.psum_scatter(
        pooled_terms.astype(jnp.bfloat16), "expert", scatter_dimension=0, tiled=True
    ).astype(jnp.float32)
    scaled = norm_gain * pooled_grad / rows_here
    cube = inv_rms * inv_rms * inv_rms
    resid_grad = inv_rms * scaled - residual * cube * jnp.mean(
        residual * scaled, axis=-1, keepdims=True
    )
    slot_grad = jnp.dot(
        place_weight,
        resid_grad,
        precision=lax.Precision.HIGHEST,
        preferred_element_type=jnp.float32,
    )
    slot_grad = slot_grad.astype(jnp.bfloat16).reshape(slot_shape)
    grad_in = lax.all_to_all(slot_grad, "expert", split_axis=0, concat_axis=0, tiled=True)
    back_list = []
    for local in range(local_experts):
        grad_rows = grad_in[:, local].reshape(-1, feature_dim)
        gate_act = gate_list[local]
        sigmoid_gate = jax.nn.sigmoid(gate_act)
        down_back = lax.dot_general(
            grad_rows,
            down_full[local],
            (((1,), (1,)), ((), ())),
            preferred_element_type=jnp.float32,
        )
        silu_slope = sigmoid_gate * (1.0 + gate_act * (1.0 - sigmoid_gate))
        gate_grad = (down_back * up_list[local] * silu_slope).astype(jnp.bfloat16)
        up_grad = (down_back * gate_act * sigmoid_gate).astype(jnp.bfloat16)
        input_grad = lax.dot_general(
            gate_grad,
            gate_full[local],
            (((1,), (1,)), ((), ())),
            preferred_element_type=jnp.float32,
        )
        input_grad = input_grad + lax.dot_general(
            up_grad, up_full[local], (((1,), (1,)), ((), ())), preferred_element_type=jnp.float32
        )
        back_list.append(
            input_grad.astype(jnp.bfloat16).reshape(expert_count, capacity, feature_dim)
        )
    input_grad_all = jnp.stack(back_list, axis=1)
    grad_back = lax.all_to_all(
        input_grad_all, "expert", split_axis=0, concat_axis=0, tiled=True
    ).reshape(-1, feature_dim)
    grad_pick = jnp.take(grad_back, slot_index.reshape(-1), axis=0).reshape(
        rows_here, top_count, feature_dim
    )
    token_grad = (resid_grad + jnp.sum(grad_pick.astype(jnp.float32), axis=1)).astype(jnp.bfloat16)
    return (token_grad, head_grad)


def solution(mesh):
    in_specs = (
        P(("rep", "expert", "group"), None),
        P("expert", "group", None),
        P("expert", "group", None),
        P("expert", "group", None),
        P(("rep", "expert", "group"), None),
        P(("rep", "expert", "group"), None),
        P(),
        P(None, "expert"),
        P("rep", "group", "expert"),
    )
    out_specs = (P(("rep", "expert", "group"), None), P("rep", "expert"))
    return jax.shard_map(body, mesh=mesh, in_specs=in_specs, out_specs=out_specs, check_vma=False)
```

profile of v0, /device:TPU:0, one launch (start us, length us, event | category | flops | bytes accessed | tf_op | source)
XLA Modules:
  0.0 371.7 jit_solution(3693473801401391951)
XLA Ops:
  7.2 1.0 slice_bitcast_fusion.41
  8.2 0.2 convert_add_fusion
  8.4 0.2 reduce_window_sum.11
  8.5 0.4 select_reduce_fusion
  9.0 0.7 multiply_add_fusion
  9.7 3.5 convolution_convert_fusion.1
  13.2 7.2 %all-to-all-start = ((bf16[8,2,80,1024]{3,2,1,0:T(8,128)(2,1)}), bf16[8,2,80,1024]{3,2,1,0:T(8,128)(2,1)S(1)}, u32[]{:S(2)}, u32[]{:S(2)}) async-start(bf16[8,2,80,1024]{3,2,1,0:T(8,128)(2,1)} %bitcast.142), calls=%async_computation | async-start | bytes 5242880 | tf_op jit(solution)/shard_map/all_to_all | solution.py:50
  20.4 0.0 all-gather.5.cloned.1.call-start
  20.5 0.7 all-gather.5.cloned.1.call-update
  21.2 0.0 all-gather.7.cloned.1.call-start
  21.2 0.7 all-gather.7.cloned.1.call-update
  21.9 0.0 all-gather.9.cloned.1.call-start
  22.0 0.7 all-gather.9.cloned.1.call-update
  22.7 57.3 %all-to-all-done = bf16[8,2,80,1024]{3,2,1,0:T(8,128)(2,1)S(1)} async-done(((bf16[8,2,80,1024]{3,2,1,0:T(8,128)(2,1)}), bf16[8,2,80,1024]{3,2,1,0:T(8,128)(2,1)S(1)}, u32[]{:S(2)}, u32[]{:S(2)}) %all-to-all-start) | async-done | bytes 2621472 | tf_op jit(solution)/shard_map/all_to_all | solution.py:50
  79.9 1.9 fusion.82
  81.8 3.4 fusion.12
  85.2 3.1 fusion.13
  88.3 1.9 fusion.17
  90.2 0.8 fusion.16
  91.0 0.0 all-gather.9.cloned.1.call-done
  91.1 3.0 convolution_convert_fusion.3
  94.1 0.9 convolution_convert_fusion.2
  95.0 1.7 pad_maximum_fusion
  96.7 3.8 %all-to-all-start.1 = ((bf16[8,2,80,1024]{3,2,1,0:T(8,128)(2,1)}), bf16[8,2,80,1024]{3,2,1,0:T(8,128)(2,1)S(1)}, u32[]{:S(2)}, u32[]{:S(2)}) async-start(bf16[8,2,80,1024]{3,2,1,0:T(8,128)(2,1)} %pad_maximum_fusion), calls=%async_computation.1 | async-start | bytes 5242880 | tf_op jit(solution)/shard_map/all_to_all | solution.py:69
  100.5 0.1 copy.18
  100.6 0.1 reshape.86
  100.7 0.1 copy.24
  100.9 0.6 dynamic-slice
  101.5 58.6 %all-to-all-done.1 = bf16[8,2,80,1024]{3,2,1,0:T(8,128)(2,1)S(1)} async-done(((bf16[8,2,80,1024]{3,2,1,0:T(8,128)(2,1)}), bf16[8,2,80,1024]{3,2,1,0:T(8,128)(2,1)S(1)}, u32[]{:S(2)}, u32[]{:S(2)}) %all-to-all-start.1) | async-done | bytes 2621472 | tf_op jit(solution)/shard_map/all_to_all | solution.py:69
  160.1 5.4 %gather_fusion = bf16[1024,1024]{1,0:T(8,128)(2,1)} fusion(bf16[1280,1024]{1,0:T(8,128)(2,1)S(1)} %bitcast.140, s32[1024]{0:T(1024)S(1)} %fusion.71), kind=kCustom, calls=%fused_computation.clone | custom fusion | bytes 4198400 | tf_op jit(solution)/shard_map/jit(_take)/gather | solution.py:72
  165.5 2.4 fusion
  167.9 0.2 multiply_reduce_fusion.2
  168.1 0.2 multiply_reduce_fusion.1
  168.3 26.0 %all-gather = bf16[8192]{0:T(1024)(128)(2,1)S(1)} all-gather(bf16[1024]{0:T(1024)(128)(2,1)S(1)} %multiply_convert_fusion.12), channel_id=2, replica_groups=mesh['rep'=2,'expert'=8,'group'=2] {'expert'}, dimensions={0}, use_global_device_ids=true | all-gather | bytes 18432 | tf_op jit(solution)/shard_map/all_gather | solution.py:80
  194.3 0.2 fusion.9
  194.5 0.2 convolution_convert_fusion.5
  194.8 33.8 %all-reduce = bf16[8,1024]{1,0:T(8,128)(2,1)S(1)} all-reduce(bf16[8,1024]{1,0:T(8,128)(2,1)S(1)} %convolution_convert_fusion.5), channel_id=3, replica_groups=mesh['rep'=2,'expert'=8,'group'=2] {'expert'}, use_global_device_ids=true, to_apply=%region_12.14.clone | all-reduce | flops 8192 | bytes 32768
  228.5 0.7 fusion.70
  229.2 0.2 multiply_reduce_fusion
  229.4 5.3 %convolution_convert_fusion = bf16[1280,1024]{1,0:T(8,128)(2,1)S(1)} fusion(f32[128]{0:T(128)S(1)} %get-tuple-element.16, f32[128]{0:T(128)S(1)} %get-tuple-element.17, f32[128]{0:T(128)S(1)} %get-tuple-element.18, f32[128]{0:T(128)S(1)} %get-tuple-element.19, f32[128]{0:T(128)S(1)} %get-tuple-element.20, f32[128]{0:T(128)S(1)} %get-tuple-element.21, ...), kind=kOutput, calls=%fused_computation.3 | convolution fusion | flops 2019131392 | bytes 3421696 | tf_op jit(solution)/shard_map/dot_general | solution.py:99
  234.7 51.1 %all_to_all.20 = bf16[8,2,80,1024]{3,2,1,0:T(8,128)(2,1)S(1)} all-to-all(bf16[8,2,80,1024]{3,2,1,0:T(8,128)(2,1)S(1)} %bitcast.143), channel_id=1, replica_groups=mesh['rep'=2,'expert'=8,'group'=2] {'expert'}, dimensions={0} | all-to-all | bytes 5242880 | tf_op jit(solution)/shard_map/all_to_all | solution.py:106
  285.8 0.4 fusion.81
  286.2 1.0 copy-done.14
  287.2 0.9 fusion.14
  288.1 0.6 copy-done.10
  288.7 0.3 copy-done.20
  288.9 1.0 fusion.11
  290.0 0.4 copy-done.12
  290.4 0.9 add_convert_fusion.1
  291.3 0.9 fusion.18
  292.2 0.3 copy-done.17
  292.5 0.3 copy-done.19
  292.8 1.0 fusion.15
  293.8 0.9 add_convert_fusion
  294.7 1.7 pad_maximum_fusion.1
  296.5 3.7 all-to-all-start.3
  300.1 0.0 all-reduce.3.cloned.1.call-start
  300.2 1.1 convolution_convert_fusion.4
  301.4 22.4 %all-reduce.3.cloned.1.call-done = bf16[1024,250]{1,0:T(8,128)(2,1)} async-done(((bf16[1024,250]{1,0:T(8,128)(2,1)}), bf16[1024,250]{1,0:T(8,128)(2,1)}) %all-reduce.3.cloned.1.call-update) | async-done | bytes 512016 | tf_op jit(solution)/shard_map/psum | solution.py:87
  323.8 2.1 convert_element_type.176
  325.9 30.0 %all-to-all-done.3 = bf16[8,2,80,1024]{3,2,1,0:T(8,128)(2,1)S(1)} async-done(((bf16[8,2,80,1024]{3,2,1,0:T(8,128)(2,1)}), bf16[8,2,80,1024]{3,2,1,0:T(8,128)(2,1)S(1)}, u32[]{:S(2)}, u32[]{:S(2)}) %all-to-all-start.3) | async-done | bytes 2621472 | tf_op jit(solution)/shard_map/all_to_all | solution.py:134
  355.9 5.4 %gather_fusion.1 = bf16[1024,1024]{1,0:T(8,128)(2,1)} fusion(bf16[1280,1024]{1,0:T(8,128)(2,1)S(1)} %bitcast.141, s32[1024]{0:T(1024)S(1)} %fusion.71), kind=kCustom, calls=%fused_computation.1.clone | custom fusion | bytes 4198400 | tf_op jit(solution)/shard_map/jit(_take)/gather | solution.py:137
  361.2 3.0 convert_reduce_fusion
  364.3 0.9 add_convert_fusion.3
  (53 shorter events, 0.2 us)
Async XLA Ops:
  7.2 187.2 %copy-start = (bf16[1024,250]{1,0:T(8,128)(2,1)S(1)}, bf16[1024,250]{1,0:T(8,128)(2,1)}, u32[]{:S(2)}) copy-start(bf16[1024,250]{1,0:T(8,128)(2,1)} %param.18) | copy-start | bytes 1536004
  13.2 66.7 %all-to-all-start = ((bf16[8,2,80,1024]{3,2,1,0:T(8,128)(2,1)}), bf16[8,2,80,1024]{3,2,1,0:T(8,128)(2,1)S(1)}, u32[]{:S(2)}, u32[]{:S(2)}) async-start(bf16[8,2,80,1024]{3,2,1,0:T(8,128)(2,1)} %bitcast.142), calls=%async_computation | async-start | bytes 5242880 | tf_op jit(solution)/shard_map/all_to_all | solution.py:50
  20.4 61.4 %all-gather.5.cloned.1.call-start = ((), (), s32[]{:S(2)}) async-start(), calls=%async_computation.4 | async-start | bytes 2359296 | tf_op jit(solution)/shard_map/all_gather | solution.py:46
  21.2 64.1 %all-gather.7.cloned.1.call-start = ((), (), s32[]{:S(2)}) async-start(), calls=%async_computation.5 | async-start | bytes 2359296 | tf_op jit(solution)/shard_map/all_gather | solution.py:47
  21.9 69.1 %all-gather.9.cloned.1.call-start = ((), (), s32[]{:S(2)}) async-start(), calls=%async_computation.6 | async-start | bytes 2359296 | tf_op jit(solution)/shard_map/all_gather | solution.py:48
  81.8 3.4 copy-start.5
  85.2 3.1 copy-start.4
  85.2 3.1 copy-start.11
  88.3 1.9 copy-start.9
  91.0 3.0 copy-start.16
  91.0 3.0 copy-start.18
  91.1 3.0 copy-start.13
  96.7 4.0 %copy-start.6 = (f32[128,8]{0,1:T(8,128)S(1)}, f32[128,8]{0,1:T(8,128)}, u32[]{:S(2)}) copy-start(f32[128,8]{0,1:T(8,128)} %param.16) | copy-start | bytes 12292
  96.7 4.2 %copy-start.15 = (u32[32]{0:T(128)S(1)}, u32[32]{0:T(128)}, u32[]{:S(2)}) copy-start(u32[32]{0:T(128)} %constant.41) | copy-start | bytes 388
  96.7 63.4 %all-to-all-start.1 = ((bf16[8,2,80,1024]{3,2,1,0:T(8,128)(2,1)}), bf16[8,2,80,1024]{3,2,1,0:T(8,128)(2,1)S(1)}, u32[]{:S(2)}, u32[]{:S(2)}) async-start(bf16[8,2,80,1024]{3,2,1,0:T(8,128)(2,1)} %pad_maximum_fusion), calls=%async_computation.1 | async-start | bytes 5242880 | tf_op jit(solution)/shard_map/all_to_all | solution.py:69
  165.5 2.4 copy-start.3
  165.5 2.6 copy-start.7
  167.9 61.5 %copy-start.1 = (f32[128,1,1024]{2,1,0:T(1,128)}, f32[128,1,1024]{2,1,0:T(1,128)S(1)}, u32[]{:S(2)}) copy-start(f32[128,1,1024]{2,1,0:T(1,128)S(1)} %fusion) | copy-start | bytes 1572868
  167.9 26.4 %copy-start.8 = (s32[8,1,250]{2,1,0:T(1,128)S(1)}, s32[8,1,250]{2,1,0:T(1,128)}, u32[]{:S(2)}) copy-start(s32[8,1,250]{2,1,0:T(1,128)} %param.19) | copy-start | bytes 24004
  285.8 1.4 copy-start.14
  285.8 2.3 copy-start.21
  287.2 1.5 copy-start.10
  287.2 1.7 copy-start.20
  288.9 1.4 copy-start.12
  291.3 1.2 copy-start.17
  291.3 1.5 copy-start.19
  296.5 59.4 %all-to-all-start.3 = ((bf16[8,2,80,1024]{3,2,1,0:T(8,128)(2,1)}), bf16[8,2,80,1024]{3,2,1,0:T(8,128)(2,1)S(1)}, u32[]{:S(2)}, u32[]{:S(2)}) async-start(bf16[8,2,80,1024]{3,2,1,0:T(8,128)(2,1)} %pad_maximum_fusion.1), calls=%async_computation.3 | async-start | bytes 5242880 | tf_op jit(solution)/shard_map/all_to_all | solution.py:134
  300.1 23.6 %all-reduce.3.cloned.1.call-start = ((), (), s32[]{:S(2)}) async-start(), calls=%async_computation.7 | async-start | bytes 1048576 | tf_op jit(solution)/shard_map/psum | solution.py:87
  361.2 3.0 copy-start.2
Sparse Core Ops, SparseCore 0:
  22.8 11.2 all-gather.4
  35.6 10.9 all-gather.6
  48.2 10.9 all-gather.8
  303.6 20.1 all-reduce.2
where the time goes:
time: 372 us
  waiting for transfers between devices  170 us (46%)
  blocking collectives  111 us (30%)
  matrix products  31.4 us (8%)
  local copies, waits for them, and re-layouts  17.9 us (5%)
  starting transfers between devices  14.8 us (4%)
  between operations  14.1 us (4%)
  other arithmetic  12.2 us (3%)
    all_to_all x1, waiting for transfers between devices, body(): lax.all_to_all(expert_out_all, 'expert', split_axis=0, concat_axis=0, til...  58.6 us
    all_to_all x1, waiting for transfers between devices, body(): lax.all_to_all(outgoing, 'expert', split_axis=0, concat_axis=0, tiled=True)  57.3 us
    all_to_all x1, blocking collectives, body(): lax.all_to_all(slot_grad, 'expert', split_axis=0, concat_axis=0, tiled=True)  51.1 us
    unnamed x1, blocking collectives  33.8 us
    all_to_all x1, waiting for transfers between devices, body(): lax.all_to_all(input_grad_all, 'expert', split_axis=0, concat_axis=0, til...  30 us
    all_gather x1, blocking collectives, body(): pooled_all = lax.all_gather(pooled, 'expert', axis=0, tiled=True)  26 us
    psum x1, waiting for transfers between devices, body(): lax.psum(head_part.astype(jnp.bfloat16), 'group').astype(jnp.float32)  22.4 us
  transfers between devices with their start and end apart: 7, of which 4 were waited for; matrix products, arithmetic and copies ran while one was open for 4% of the time, Pallas kernels for 0%

commit v1 on v0

--- a/solution.py
+++ b/solution.py
@@ -77,7 +77,14 @@
     inv_rms = lax.rsqrt(jnp.mean(residual * residual, axis=-1, keepdims=True) + NORM_EPS)
     normed = residual * inv_rms * norm_gain
     pooled = jnp.mean(normed, axis=0, keepdims=True).astype(jnp.bfloat16)
-    pooled_all = lax.all_gather(pooled, "expert", axis=0, tiled=True)
+    ring = [pooled]
+    for hop in range(7):
+        ring.append(lax.ppermute(ring[-1], "expert", [(dev, (dev + 1) % 8) for dev in range(8)]))
+    pooled_all = jnp.roll(
+        jnp.concatenate(ring[::-1], axis=0),
+        (lax.axis_index("expert") + 1) * ring[0].shape[0],
+        axis=0,
+    )
     logits = jnp.dot(pooled_all, class_head, preferred_element_type=jnp.float32)
     target_rows = targets.reshape(expert_count, -1).astype(jnp.float32)
     logit_grad = (LOSS_SCALE * (jax.nn.sigmoid(logits) - target_rows)).astype(jnp.bfloat16)

time: 372 us -> 384 us (1.032)
  waiting for transfers between devices: 170 us -> 212 us
  blocking collectives: 111 us -> 79.5 us
    ppermute x0 -> x7, waiting for transfers between devices: none -> 42 us  [body(): lax.ppermute(ring[-1], 'expert', [(dev, (dev + 1) % 8) for dev in range(8)])]
    all_gather x1 -> x0, blocking collectives: 26 us -> none  [body(): pooled_all = lax.all_gather(pooled, 'expert', axis=0, tiled=True)]
    all_to_all x1, blocking collectives: 51.1 us -> 46 us  [body(): lax.all_to_all(slot_grad, 'expert', split_axis=0, concat_axis=0, tiled=True)]
  transfers between devices with their start and end apart: 7 -> 14, of which waited for: 4 -> 11; matrix products, arithmetic and copies ran while one was open for 4% -> 4% of each run, Pallas kernels for 0% -> 0%
where the time goes in v1:
time: 384 us; the launch traced here: 383 us
  waiting for transfers between devices  212 us (55%)
  blocking collectives  79.5 us (21%)
  matrix products  31.5 us (8%)
  local copies, waits for them, and re-layouts  18 us (5%)
  starting transfers between devices  16.3 us (4%)
  between operations  14.1 us (4%)
  other arithmetic  12.2 us (3%)
    all_to_all x1, waiting for transfers between devices, body(): lax.all_to_all(expert_out_all, 'expert', split_axis=0, concat_axis=0, til...  59.2 us
    all_to_all x1, waiting for transfers between devices, body(): lax.all_to_all(outgoing, 'expert', split_axis=0, concat_axis=0, tiled=True)  57.3 us
    all_to_all x1, blocking collectives, body(): lax.all_to_all(slot_grad, 'expert', split_axis=0, concat_axis=0, tiled=True)  46 us
    ppermute x7, waiting for transfers between devices, body(): lax.ppermute(ring[-1], 'expert', [(dev, (dev + 1) % 8) for dev in range(8)])  42 us
    unnamed x1, blocking collectives  33.4 us
    all_to_all x1, waiting for transfers between devices, body(): lax.all_to_all(input_grad_all, 'expert', split_axis=0, concat_axis=0, til...  28.5 us
    psum x1, waiting for transfers between devices, body(): lax.psum(head_part.astype(jnp.bfloat16), 'group').astype(jnp.float32)  22.4 us
  transfers between devices with their start and end apart: 14, of which 11 were waited for; matrix products, arithmetic and copies ran while one was open for 4% of the time, Pallas kernels for 0%

profile of v1, /device:TPU:0, one launch (start us, length us, event | category | flops | bytes accessed | tf_op | source)
XLA Modules:
  0.0 383.1 jit_solution(7884018732679930614)
XLA Ops:
  7.2 1.0 slice_bitcast_fusion.41
  8.2 0.2 convert_add_fusion
  8.4 0.2 reduce_window_sum.11
  8.5 0.4 select_reduce_fusion
  9.0 0.7 multiply_add_fusion
  9.7 3.6 convolution_convert_fusion.1
  13.2 7.2 %all-to-all-start = ((bf16[8,2,80,1024]{3,2,1,0:T(8,128)(2,1)}), bf16[8,2,80,1024]{3,2,1,0:T(8,128)(2,1)S(1)}, u32[]{:S(2)}, u32[]{:S(2)}) async-start(bf16[8,2,80,1024]{3,2,1,0:T(8,128)(2,1)} %bitcast.140), calls=%async_computation | async-start | bytes 5242880 | tf_op jit(solution)/shard_map/all_to_all | solution.py:50
  20.5 0.7 all-gather.4.cloned.1.call-update
  21.2 0.7 all-gather.6.cloned.1.call-update
  22.0 0.7 all-gather.8.cloned.1.call-update
  22.7 57.3 %all-to-all-done = bf16[8,2,80,1024]{3,2,1,0:T(8,128)(2,1)S(1)} async-done(((bf16[8,2,80,1024]{3,2,1,0:T(8,128)(2,1)}), bf16[8,2,80,1024]{3,2,1,0:T(8,128)(2,1)S(1)}, u32[]{:S(2)}, u32[]{:S(2)}) %all-to-all-start) | async-done | bytes 2621472 | tf_op jit(solution)/shard_map/all_to_all | solution.py:50
  79.9 1.9 fusion.86
  81.8 3.4 fusion.12
  85.3 3.1 fusion.13
  88.4 1.9 fusion.17
  90.3 0.8 fusion.16
  91.2 3.0 convolution_convert_fusion.3
  94.2 0.9 convolution_convert_fusion.2
  95.1 1.8 pad_maximum_fusion
  96.8 3.8 all-to-all-start.1
  100.8 0.1 copy.24
  101.0 59.2 %all-to-all-done.1 = bf16[8,2,80,1024]{3,2,1,0:T(8,128)(2,1)S(1)} async-done(((bf16[8,2,80,1024]{3,2,1,0:T(8,128)(2,1)}), bf16[8,2,80,1024]{3,2,1,0:T(8,128)(2,1)S(1)}, u32[]{:S(2)}, u32[]{:S(2)}) %all-to-all-start.1) | async-done | bytes 2621472 | tf_op jit(solution)/shard_map/all_to_all | solution.py:69
  160.2 5.3 %gather_fusion = bf16[1024,1024]{1,0:T(8,128)(2,1)} fusion(bf16[1280,1024]{1,0:T(8,128)(2,1)S(1)} %bitcast.139, s32[1024]{0:T(1024)S(1)} %fusion.73), kind=kCustom, calls=%fused_computation.clone | custom fusion | bytes 4198400 | tf_op jit(solution)/shard_map/jit(_take)/gather | solution.py:72
  165.6 2.4 fusion
  168.1 0.2 multiply_reduce_fusion.2
  168.2 0.2 multiply_reduce_fusion.1
  168.4 1.5 collective-permute-start
  169.9 4.8 %collective-permute-done = bf16[1,1024]{1,0:T(2,128)(2,1)S(1)} collective-permute-done((bf16[1,1024]{1,0:T(2,128)(2,1)S(1)}, bf16[1,1024]{1,0:T(2,128)(2,1)S(1)}, u32[]{:S(2)}, u32[]{:S(2)}) %collective-permute-start) | collective-permute-done | bytes 2080 | tf_op jit(solution)/shard_map/ppermute | solution.py:82
  174.8 6.3 %collective-permute-done.1 = bf16[1,1024]{1,0:T(2,128)(2,1)S(1)} collective-permute-done((bf16[1,1024]{1,0:T(2,128)(2,1)S(1)}, bf16[1,1024]{1,0:T(2,128)(2,1)S(1)}, u32[]{:S(2)}, u32[]{:S(2)}) %collective-permute-start.1) | collective-permute-done | bytes 2080 | tf_op jit(solution)/shard_map/ppermute | solution.py:82
  181.1 6.3 %collective-permute-done.2 = bf16[1,1024]{1,0:T(2,128)(2,1)S(1)} collective-permute-done((bf16[1,1024]{1,0:T(2,128)(2,1)S(1)}, bf16[1,1024]{1,0:T(2,128)(2,1)S(1)}, u32[]{:S(2)}, u32[]{:S(2)}) %collective-permute-start.2) | collective-permute-done | bytes 2080 | tf_op jit(solution)/shard_map/ppermute | solution.py:82
  187.4 6.3 %collective-permute-done.3 = bf16[1,1024]{1,0:T(2,128)(2,1)S(1)} collective-permute-done((bf16[1,1024]{1,0:T(2,128)(2,1)S(1)}, bf16[1,1024]{1,0:T(2,128)(2,1)S(1)}, u32[]{:S(2)}, u32[]{:S(2)}) %collective-permute-start.3) | collective-permute-done | bytes 2080 | tf_op jit(solution)/shard_map/ppermute | solution.py:82
  193.7 6.3 %collective-permute-done.4 = bf16[1,1024]{1,0:T(2,128)(2,1)S(1)} collective-permute-done((bf16[1,1024]{1,0:T(2,128)(2,1)S(1)}, bf16[1,1024]{1,0:T(2,128)(2,1)S(1)}, u32[]{:S(2)}, u32[]{:S(2)}) %collective-permute-start.4) | collective-permute-done | bytes 2080 | tf_op jit(solution)/shard_map/ppermute | solution.py:82
  200.0 6.3 %collective-permute-done.5 = bf16[1,1024]{1,0:T(2,128)(2,1)S(1)} collective-permute-done((bf16[1,1024]{1,0:T(2,128)(2,1)S(1)}, bf16[1,1024]{1,0:T(2,128)(2,1)S(1)}, u32[]{:S(2)}, u32[]{:S(2)}) %collective-permute-start.5) | collective-permute-done | bytes 2080 | tf_op jit(solution)/shard_map/ppermute | solution.py:82
  206.4 0.6 dynamic-slice
  206.9 5.7 %collective-permute-done.6 = bf16[1,1024]{1,0:T(2,128)(2,1)S(1)} collective-permute-done((bf16[1,1024]{1,0:T(2,128)(2,1)S(1)}, bf16[1,1024]{1,0:T(2,128)(2,1)S(1)}, u32[]{:S(2)}, u32[]{:S(2)}) %collective-permute-start.6) | collective-permute-done | bytes 2080 | tf_op jit(solution)/shard_map/ppermute | solution.py:82
  212.8 0.2 fusion.9
  213.0 0.2 convolution_convert_fusion.5
  213.2 33.4 %all-reduce = bf16[8,1024]{1,0:T(8,128)(2,1)S(1)} all-reduce(bf16[8,1024]{1,0:T(8,128)(2,1)S(1)} %convolution_convert_fusion.5), channel_id=2, replica_groups=mesh['rep'=2,'expert'=8,'group'=2] {'expert'}, use_global_device_ids=true, to_apply=%region_12.14.clone | all-reduce | flops 8192 | bytes 32768
  246.6 0.7 fusion.72
  247.2 0.2 multiply_reduce_fusion
  247.4 5.3 %convolution_convert_fusion = bf16[1280,1024]{1,0:T(8,128)(2,1)S(1)} fusion(f32[128]{0:T(128)S(1)} %get-tuple-element.16, f32[128]{0:T(128)S(1)} %get-tuple-element.17, f32[128]{0:T(128)S(1)} %get-tuple-element.18, f32[128]{0:T(128)S(1)} %get-tuple-element.19, f32[128]{0:T(128)S(1)} %get-tuple-element.20, f32[128]{0:T(128)S(1)} %get-tuple-element.21, ...), kind=kOutput, calls=%fused_computation.3 | convolution fusion | flops 2019131392 | bytes 3421696 | tf_op jit(solution)/shard_map/dot_general | solution.py:106
  252.7 46.0 %all_to_all.20 = bf16[8,2,80,1024]{3,2,1,0:T(8,128)(2,1)S(1)} all-to-all(bf16[8,2,80,1024]{3,2,1,0:T(8,128)(2,1)S(1)} %bitcast.141), channel_id=1, replica_groups=mesh['rep'=2,'expert'=8,'group'=2] {'expert'}, dimensions={0} | all-to-all | bytes 5242880 | tf_op jit(solution)/shard_map/all_to_all | solution.py:113
  298.8 0.4 fusion.85
  299.1 1.0 copy-done.14
  300.2 0.9 fusion.14
  301.0 0.6 copy-done.10
  301.6 0.3 copy-done.20
  301.9 1.0 fusion.11
  303.0 0.4 copy-done.12
  303.3 0.9 add_convert_fusion.1
  304.3 0.9 fusion.18
  305.1 0.3 copy-done.17
  305.4 0.3 copy-done.19
  305.7 1.0 fusion.15
  306.8 0.9 add_convert_fusion
  307.7 1.8 pad_maximum_fusion.1
  309.4 3.6 all-to-all-start.3
  313.1 1.2 convolution_convert_fusion.4
  314.3 22.4 %all-reduce.3.cloned.1.call-done = bf16[1024,250]{1,0:T(8,128)(2,1)} async-done(((bf16[1024,250]{1,0:T(8,128)(2,1)}), bf16[1024,250]{1,0:T(8,128)(2,1)}) %all-reduce.3.cloned.1.call-update) | async-done | bytes 512016 | tf_op jit(solution)/shard_map/psum | solution.py:94
  336.7 2.1 convert_element_type.176
  338.8 28.5 %all-to-all-done.3 = bf16[8,2,80,1024]{3,2,1,0:T(8,128)(2,1)S(1)} async-done(((bf16[8,2,80,1024]{3,2,1,0:T(8,128)(2,1)}), bf16[8,2,80,1024]{3,2,1,0:T(8,128)(2,1)S(1)}, u32[]{:S(2)}, u32[]{:S(2)}) %all-to-all-start.3) | async-done | bytes 2621472 | tf_op jit(solution)/shard_map/all_to_all | solution.py:141
  367.3 5.3 %gather_fusion.1 = bf16[1024,1024]{1,0:T(8,128)(2,1)} fusion(bf16[1280,1024]{1,0:T(8,128)(2,1)S(1)} %bitcast.138, s32[1024]{0:T(1024)S(1)} %fusion.73), kind=kCustom, calls=%fused_computation.1.clone | custom fusion | bytes 4198400 | tf_op jit(solution)/shard_map/jit(_take)/gather | solution.py:144
  372.7 3.0 convert_reduce_fusion
  375.7 0.9 add_convert_fusion.3
  (67 shorter events, 0.7 us)
Async XLA Ops:
  7.2 205.6 %copy-start = (bf16[1024,250]{1,0:T(8,128)(2,1)S(1)}, bf16[1024,250]{1,0:T(8,128)(2,1)}, u32[]{:S(2)}) copy-start(bf16[1024,250]{1,0:T(8,128)(2,1)} %param.18) | copy-start | bytes 1536004
  13.2 66.7 %all-to-all-start = ((bf16[8,2,80,1024]{3,2,1,0:T(8,128)(2,1)}), bf16[8,2,80,1024]{3,2,1,0:T(8,128)(2,1)S(1)}, u32[]{:S(2)}, u32[]{:S(2)}) async-start(bf16[8,2,80,1024]{3,2,1,0:T(8,128)(2,1)} %bitcast.140), calls=%async_computation | async-start | bytes 5242880 | tf_op jit(solution)/shard_map/all_to_all | solution.py:50
  20.5 61.4 %all-gather.4.cloned.1.call-start = ((), (), s32[]{:S(2)}) async-start(), calls=%async_computation.4 | async-start | bytes 2359296 | tf_op jit(solution)/shard_map/all_gather | solution.py:46
  21.2 64.1 %all-gather.6.cloned.1.call-start = ((), (), s32[]{:S(2)}) async-start(), calls=%async_computation.5 | async-start | bytes 2359296 | tf_op jit(solution)/shard_map/all_gather | solution.py:47
  21.9 69.2 %all-gather.8.cloned.1.call-start = ((), (), s32[]{:S(2)}) async-start(), calls=%async_computation.6 | async-start | bytes 2359296 | tf_op jit(solution)/shard_map/all_gather | solution.py:48
  81.8 3.5 copy-start.5
  85.3 3.1 copy-start.4
  85.3 3.1 copy-start.11
  88.4 1.9 copy-start.9
  91.1 3.0 copy-start.16
  91.1 3.0 copy-start.18
  91.2 3.0 copy-start.13
  96.8 4.0 %copy-start.6 = (f32[128,8]{0,1:T(8,128)S(1)}, f32[128,8]{0,1:T(8,128)}, u32[]{:S(2)}) copy-start(f32[128,8]{0,1:T(8,128)} %param.16) | copy-start | bytes 12292
  96.8 63.4 %all-to-all-start.1 = ((bf16[8,2,80,1024]{3,2,1,0:T(8,128)(2,1)}), bf16[8,2,80,1024]{3,2,1,0:T(8,128)(2,1)S(1)}, u32[]{:S(2)}, u32[]{:S(2)}) async-start(bf16[8,2,80,1024]{3,2,1,0:T(8,128)(2,1)} %pad_maximum_fusion), calls=%async_computation.1 | async-start | bytes 5242880 | tf_op jit(solution)/shard_map/all_to_all | solution.py:69
  165.6 2.4 copy-start.3
  165.6 2.7 copy-start.7
  168.0 79.4 %copy-start.1 = (f32[128,1,1024]{2,1,0:T(1,128)}, f32[128,1,1024]{2,1,0:T(1,128)S(1)}, u32[]{:S(2)}) copy-start(f32[128,1,1024]{2,1,0:T(1,128)S(1)} %fusion) | copy-start | bytes 1572868
  168.0 38.3 %copy-start.15 = (u32[32]{0:T(128)S(1)}, u32[32]{0:T(128)}, u32[]{:S(2)}) copy-start(u32[32]{0:T(128)} %constant.70) | copy-start | bytes 388
  168.0 44.7 %copy-start.8 = (s32[8,1,250]{2,1,0:T(1,128)S(1)}, s32[8,1,250]{2,1,0:T(1,128)}, u32[]{:S(2)}) copy-start(s32[8,1,250]{2,1,0:T(1,128)} %param.19) | copy-start | bytes 24004
  168.4 6.4 %collective-permute-start = (bf16[1,1024]{1,0:T(2,128)(2,1)S(1)}, bf16[1,1024]{1,0:T(2,128)(2,1)S(1)}, u32[]{:S(2)}, u32[]{:S(2)}) collective-permute-start(bf16[1,1024]{1,0:T(2,128)(2,1)S(1)} %convert_element_type.159), channel_id=1, source_target_pairs={{0,2},{2,4},{4,6},{6,8},{8,10},{10,12},{12,14},{14,0},{1,3},{3,5},... | collective-permute-start | bytes 6152 | tf_op jit(solution)/shard_map/ppermute | solution.py:82
  174.8 6.3 %collective-permute-start.1 = (bf16[1,1024]{1,0:T(2,128)(2,1)S(1)}, bf16[1,1024]{1,0:T(2,128)(2,1)S(1)}, u32[]{:S(2)}, u32[]{:S(2)}) collective-permute-start(bf16[1,1024]{1,0:T(2,128)(2,1)S(1)} %collective-permute-done), channel_id=1, source_target_pairs={{0,2},{2,4},{4,6},{6,8},{8,10},{10,12},{12,14},{14,0},{1,3},{3,5},... | collective-permute-start | bytes 6152 | tf_op jit(solution)/shard_map/ppermute | solution.py:82
  181.1 6.3 %collective-permute-start.2 = (bf16[1,1024]{1,0:T(2,128)(2,1)S(1)}, bf16[1,1024]{1,0:T(2,128)(2,1)S(1)}, u32[]{:S(2)}, u32[]{:S(2)}) collective-permute-start(bf16[1,1024]{1,0:T(2,128)(2,1)S(1)} %collective-permute-done.1), channel_id=1, source_target_pairs={{0,2},{2,4},{4,6},{6,8},{8,10},{10,12},{12,14},{14,0},{1,3},{3,5},... | collective-permute-start | bytes 6152 | tf_op jit(solution)/shard_map/ppermute | solution.py:82
  187.4 6.3 %collective-permute-start.3 = (bf16[1,1024]{1,0:T(2,128)(2,1)S(1)}, bf16[1,1024]{1,0:T(2,128)(2,1)S(1)}, u32[]{:S(2)}, u32[]{:S(2)}) collective-permute-start(bf16[1,1024]{1,0:T(2,128)(2,1)S(1)} %collective-permute-done.2), channel_id=1, source_target_pairs={{0,2},{2,4},{4,6},{6,8},{8,10},{10,12},{12,14},{14,0},{1,3},{3,5},... | collective-permute-start | bytes 6152 | tf_op jit(solution)/shard_map/ppermute | solution.py:82
  193.7 6.3 %collective-permute-start.4 = (bf16[1,1024]{1,0:T(2,128)(2,1)S(1)}, bf16[1,1024]{1,0:T(2,128)(2,1)S(1)}, u32[]{:S(2)}, u32[]{:S(2)}) collective-permute-start(bf16[1,1024]{1,0:T(2,128)(2,1)S(1)} %collective-permute-done.3), channel_id=1, source_target_pairs={{0,2},{2,4},{4,6},{6,8},{8,10},{10,12},{12,14},{14,0},{1,3},{3,5},... | collective-permute-start | bytes 6152 | tf_op jit(solution)/shard_map/ppermute | solution.py:82
  200.0 6.3 %collective-permute-start.5 = (bf16[1,1024]{1,0:T(2,128)(2,1)S(1)}, bf16[1,1024]{1,0:T(2,128)(2,1)S(1)}, u32[]{:S(2)}, u32[]{:S(2)}) collective-permute-start(bf16[1,1024]{1,0:T(2,128)(2,1)S(1)} %collective-permute-done.4), channel_id=1, source_target_pairs={{0,2},{2,4},{4,6},{6,8},{8,10},{10,12},{12,14},{14,0},{1,3},{3,5},... | collective-permute-start | bytes 6152 | tf_op jit(solution)/shard_map/ppermute | solution.py:82
  206.3 6.3 %collective-permute-start.6 = (bf16[1,1024]{1,0:T(2,128)(2,1)S(1)}, bf16[1,1024]{1,0:T(2,128)(2,1)S(1)}, u32[]{:S(2)}, u32[]{:S(2)}) collective-permute-start(bf16[1,1024]{1,0:T(2,128)(2,1)S(1)} %collective-permute-done.5), channel_id=1, source_target_pairs={{0,2},{2,4},{4,6},{6,8},{8,10},{10,12},{12,14},{14,0},{1,3},{3,5},... | collective-permute-start | bytes 6152 | tf_op jit(solution)/shard_map/ppermute | solution.py:82
  298.8 1.4 copy-start.14
  298.8 2.3 copy-start.21
  300.2 1.5 copy-start.10
  300.2 1.7 copy-start.20
  301.9 1.4 copy-start.12
  304.2 1.2 copy-start.17
  304.2 1.5 copy-start.19
  309.4 57.9 %all-to-all-start.3 = ((bf16[8,2,80,1024]{3,2,1,0:T(8,128)(2,1)}), bf16[8,2,80,1024]{3,2,1,0:T(8,128)(2,1)S(1)}, u32[]{:S(2)}, u32[]{:S(2)}) async-start(bf16[8,2,80,1024]{3,2,1,0:T(8,128)(2,1)} %pad_maximum_fusion.1), calls=%async_computation.3 | async-start | bytes 5242880 | tf_op jit(solution)/shard_map/all_to_all | solution.py:141
  313.1 23.6 %all-reduce.3.cloned.1.call-start = ((), (), s32[]{:S(2)}) async-start(), calls=%async_computation.7 | async-start | bytes 1048576 | tf_op jit(solution)/shard_map/psum | solution.py:94
  372.7 3.0 copy-start.2
Sparse Core Ops, SparseCore 0:
  22.8 11.2 all-gather.3
  35.7 10.9 all-gather.5
  48.2 10.9 all-gather.7
  316.5 20.1 all-reduce.2
